TPU v7x, 32 devices: a whole 2x2x4 slice. The times are simulated.
32 devices in a mesh: leaf: 8 (over z, x), sub: 4 (over y, core).
Axes of the slice: x: 2, y: 2, z: 4, core: 2. Of those that a mesh axis runs over, the one named last changes fastest.
Arguments:
- leaf_right: bfloat16 [128, 512, 256], P(('leaf', 'sub')), may hold values from -6 to 6
- leaf_inverse: bfloat16 [128, 512, 512], P(('leaf', 'sub')), may hold values from -2.5 to 2.5, as said below
- panels: bfloat16 [128, 256, 512], P(('leaf', 'sub')), may hold values from -0.125 to 0.125
- leaf_subtree: int32 [128], P(('leaf', 'sub')), may hold values from 0 to 7, as said below
- panel_block: int32 [128, 4], P(('leaf', 'sub')), may hold values from 0 to 63
- separator_right: bfloat16 [32768, 256], P(('leaf', 'sub')), may hold values from -6 to 6
- separator_inverse: bfloat16 [32768, 512], P(('leaf', 'sub')), may hold values from -2.5 to 2.5, as said below
- separator_factor: bfloat16 [32768, 4096], P(('leaf', 'sub')), may hold values from -1 to 1, as said below
Outputs:
- leaf_solution: bfloat16 [128, 512, 256], P(('leaf', 'sub'))
- separator_solution: bfloat16 [32768, 256], P(('leaf', 'sub'))
Inputs may be any that keep to these rules, and one draw needn't show every extreme that they name: `leaf_subtree`: every leaf supernode held by section s of the leaf axis belongs to a subtree between s - (2) and s. Each device of section s holds, for every d from 0 to min(2, s), at least one leaf supernode of subtree s - d. `leaf_inverse`: each 512 x 512 block is lower triangular, with its diagonal between 0.6 and 1.4. `separator_inverse`: each 512 x 512 block is lower triangular, with its diagonal between 0.6 and 1.4. `separator_factor`: within each subtree's 4096 rows, the block of row block q and column block p (blocks of 512) is zero unless q > p.
All inputs are finite; a program needn't handle non-finite values.
Results may differ from a plain program's by a relative error of at most 0.024.
Values may be sent and summed in bfloat16 or wider, within the bound.
A program may use at most 128 MiB of HBM per device.

v0:
```python
import jax
import jax.numpy as jnp
from jax import lax
from jax.sharding import PartitionSpec as P

WSN = 512
SA = 4096
R = 256
BLK = 64
KB = 4
SPAN = 3


exact_precision = lax.Precision.HIGHEST


def passed_along(block, axis, distance):
    devices = range(lax.axis_size(axis))
    route = [(i - distance, i) for i in devices if i - distance in devices]
    return lax.ppermute(block, axis, route)


def broadcast(shard, axis, root):
    mine = lax.axis_index(axis) == root
    return lax.psum(jnp.where(mine, shard, jnp.zeros_like(shard)), axis)


def route_forward(stacked):
    summed = stacked[0]
    for distance in range(1, SPAN):
        summed = summed + passed_along(stacked[distance], "leaf", -distance)
    return summed


def route_back(item):
    collected = [item] + [passed_along(item, "leaf", distance) for distance in range(1, SPAN)]
    return jnp.stack(collected)


def shards(
    leaf_right,
    leaf_inverse,
    panels,
    leaf_subtree,
    panel_block,
    separator_right,
    separator_inverse,
    separator_factor,
):
    section = lax.axis_index("leaf")
    member = lax.axis_index("sub")
    leaves_here = leaf_right.shape[0]
    row_blocks = SA // BLK
    share_rows = separator_right.shape[0]
    per_device = share_rows // WSN
    solved = jnp.einsum(
        "jab,jbr->jar", leaf_inverse, leaf_right, preferred_element_type=jnp.float32
    ).astype(jnp.bfloat16)
    updates = jnp.einsum(
        "jib,jbr->jir", panels, solved, preferred_element_type=jnp.float32
    ).reshape(leaves_here * KB, BLK * R)
    offsets = section - leaf_subtree
    slot_index = (offsets[:, None] * row_blocks + panel_block).reshape(-1)
    selector = (
        jnp.arange(SPAN * row_blocks, dtype=jnp.int32)[:, None] == slot_index[None, :]
    ).astype(jnp.float32)
    spilled = jnp.dot(
        selector, updates, precision=exact_precision, preferred_element_type=jnp.float32
    ).reshape(SPAN, SA, R)
    own_rows = lax.psum_scatter(route_forward(spilled), "sub", scatter_dimension=0, tiled=True)
    rhs_rows = (separator_right.astype(jnp.float32) - own_rows).astype(jnp.bfloat16)
    inverse_blocks = separator_inverse.reshape(per_device, WSN, WSN)
    running = rhs_rows.astype(jnp.float32).reshape(per_device, WSN, R)
    empty_block = jnp.zeros((WSN, R), jnp.bfloat16)
    forward_store = jnp.zeros((per_device, WSN, R), jnp.bfloat16)
    for column in range(SA // WSN):
        owner = column // per_device
        local_col = column % per_device
        is_owner = member == owner

        def solve_block():
            return jnp.dot(
                inverse_blocks[local_col].astype(jnp.float32),
                running[local_col],
                precision=exact_precision,
                preferred_element_type=jnp.float32,
            ).astype(jnp.bfloat16)

        own_block = lax.cond(is_owner, solve_block, lambda: empty_block)
        block_y = broadcast(own_block, "sub", owner)
        forward_store = forward_store.at[local_col].set(
            jnp.where(is_owner, block_y, forward_store[local_col])
        )
        column_panel = separator_factor[:, column * WSN : (column + 1) * WSN]
        running = running - jnp.dot(
            column_panel, block_y, preferred_element_type=jnp.float32
        ).reshape(per_device, WSN, R)
    backward_store = jnp.zeros((per_device, WSN, R), jnp.bfloat16)
    for column in reversed(range(SA // WSN)):
        owner = column // per_device
        local_col = column % per_device
        is_owner = member == owner
        column_panel = separator_factor[:, column * WSN : (column + 1) * WSN]
        partial_term = lax.dot_general(
            column_panel,
            backward_store.reshape(share_rows, R),
            (((0,), (0,)), ((), ())),
            preferred_element_type=jnp.float32,
        )
        summed_later = lax.psum(partial_term, "sub")

        def back_block():
            bracket = forward_store[local_col].astype(jnp.float32) - summed_later
            return lax.dot_general(
                inverse_blocks[local_col].astype(jnp.float32),
                bracket,
                (((0,), (0,)), ((), ())),
                precision=exact_precision,
                preferred_element_type=jnp.float32,
            ).astype(jnp.bfloat16)

        own_back = lax.cond(is_owner, back_block, lambda: empty_block)
        backward_store = backward_store.at[local_col].set(
            jnp.where(is_owner, own_back, backward_store[local_col])
        )
    separator_x = backward_store.reshape(share_rows, R)
    solution_table = route_back(lax.all_gather(separator_x, "sub", axis=0, tiled=True))
    pieces = jnp.take(solution_table.reshape(SPAN * row_blocks, BLK * R), slot_index, axis=0)
    pieces = pieces.reshape(leaves_here, KB * BLK, R)
    reduced = jnp.einsum("jib,jir->jbr", panels, pieces, preferred_element_type=jnp.float32)
    inner_rhs = (solved.astype(jnp.float32) - reduced).astype(jnp.bfloat16)
    leaf_x = jnp.einsum(
        "jab,jar->jbr", leaf_inverse, inner_rhs, preferred_element_type=jnp.float32
    ).astype(jnp.bfloat16)
    return (leaf_x, separator_x)


def solution(mesh):
    placed = (
        P(("leaf", "sub"), None, None),
        P(("leaf", "sub"), None, None),
        P(("leaf", "sub"), None, None),
        P(("leaf", "sub")),
        P(("leaf", "sub"), None),
        P(("leaf", "sub"), None),
        P(("leaf", "sub"), None),
        P(("leaf", "sub"), None),
    )
    return jax.shard_map(
        shards,
        mesh=mesh,
        in_specs=placed,
        out_specs=(P(("leaf", "sub"), None, None), P(("leaf", "sub"), None)),
        check_vma=False,
    )
```

profile of v0, /device:TPU:10, one launch (start us, length us, event | category | flops | bytes accessed | tf_op | source)
XLA Modules:
  0.0 1101.8 jit_solution(2217574592786535673)
XLA Ops:
  16.3 7.9 fusion.130
  24.2 9.4 fusion.136
  33.6 5.0 squeeze.124
  41.0 5.0 squeeze.125
  47.9 4.9 squeeze.123
  52.8 82.3 %collective-permute-done = f32[4096,256]{1,0:T(8,128)} collective-permute-done((f32[4096,256]{1,0:T(8,128)}, f32[4096,256]{1,0:T(8,128)}, u32[]{:S(2)}, u32[]{:S(2)}) %collective-permute-start) | collective-permute-done | bytes 4194336 | tf_op jit(solution)/shard_map/ppermute | solution.py:20
  135.1 5.1 collective-permute-done.1
  140.2 7.4 add_add_fusion
  147.7 127.5 %reduce-scatter.2.cloned.1.call-done = f32[1024,256]{1,0:T(8,128)} async-done(((f32[4096,256]{1,0:T(8,128)}), f32[1024,256]{1,0:T(8,128)}) %reduce-scatter.2.cloned.1.call-update) | async-done | bytes 1048592 | tf_op jit(solution)/shard_map/reduce_scatter | solution.py:70
  281.1 32.1 %all-reduce.18.cloned.1.call-done = bf16[512,256]{1,0:T(8,128)(2,1)} async-done(((bf16[512,256]{1,0:T(8,128)(2,1)}), bf16[512,256]{1,0:T(8,128)(2,1)}) %all-reduce.18.cloned.1.call-update) | async-done | bytes 262160 | tf_op jit(solution)/shard_map/psum | solution.py:25
  313.1 2.8 convolution_bitcast_fusion.6
  316.0 2.6 copy.74
  318.5 2.5 convert_subtract_fusion.16
  323.5 32.1 %all-reduce.20.cloned.1.call-done = bf16[512,256]{1,0:T(8,128)(2,1)} async-done(((bf16[512,256]{1,0:T(8,128)(2,1)}), bf16[512,256]{1,0:T(8,128)(2,1)}) %all-reduce.20.cloned.1.call-update) | async-done | bytes 262160 | tf_op jit(solution)/shard_map/psum | solution.py:25
  355.6 2.8 convolution_bitcast_fusion.5
  358.3 2.6 copy.75
  360.9 2.7 sub.62
  364.4 32.1 %all-reduce.22.cloned.1.call-done = bf16[512,256]{1,0:T(8,128)(2,1)} async-done(((bf16[512,256]{1,0:T(8,128)(2,1)}), bf16[512,256]{1,0:T(8,128)(2,1)}) %all-reduce.22.cloned.1.call-update) | async-done | bytes 262160 | tf_op jit(solution)/shard_map/psum | solution.py:25
  396.5 2.8 convolution_bitcast_fusion.4
  399.3 2.6 copy.76
  401.8 2.7 sub.63
  405.5 32.1 %all-reduce.24.cloned.1.call-done = bf16[512,256]{1,0:T(8,128)(2,1)} async-done(((bf16[512,256]{1,0:T(8,128)(2,1)}), bf16[512,256]{1,0:T(8,128)(2,1)}) %all-reduce.24.cloned.1.call-update) | async-done | bytes 262160 | tf_op jit(solution)/shard_map/psum | solution.py:25
  437.6 2.8 convolution_bitcast_fusion.3
  440.4 2.6 copy.77
  442.9 2.7 sub.64
  446.5 33.6 %all-reduce.26.cloned.1.call-done = bf16[512,256]{1,0:T(8,128)(2,1)} async-done(((bf16[512,256]{1,0:T(8,128)(2,1)}), bf16[512,256]{1,0:T(8,128)(2,1)}) %all-reduce.26.cloned.1.call-update) | async-done | bytes 262160 | tf_op jit(solution)/shard_map/psum | solution.py:25
  480.0 2.8 convolution_bitcast_fusion.2
  482.8 2.6 copy.78
  485.4 2.7 sub.65
  488.9 33.6 %all-reduce.28.cloned.1.call-done = bf16[512,256]{1,0:T(8,128)(2,1)} async-done(((bf16[512,256]{1,0:T(8,128)(2,1)}), bf16[512,256]{1,0:T(8,128)(2,1)}) %all-reduce.28.cloned.1.call-update) | async-done | bytes 262160 | tf_op jit(solution)/shard_map/psum | solution.py:25
  522.5 2.8 convolution_bitcast_fusion.1
  525.3 2.6 copy.79
  527.8 2.7 sub.66
  532.0 33.4 %all-reduce.30.cloned.1.call-done = bf16[512,256]{1,0:T(8,128)(2,1)} async-done(((bf16[512,256]{1,0:T(8,128)(2,1)}), bf16[512,256]{1,0:T(8,128)(2,1)}) %all-reduce.30.cloned.1.call-update) | async-done | bytes 262160 | tf_op jit(solution)/shard_map/psum | solution.py:25
  565.4 2.8 convolution_bitcast_fusion
  569.8 2.5 convolution_bitcast_fusion.15
  581.9 26.1 %all-reduce.32.cloned.1.call-done = bf16[512,256]{1,0:T(8,128)(2,1)} async-done(((bf16[512,256]{1,0:T(8,128)(2,1)}), bf16[512,256]{1,0:T(8,128)(2,1)}) %all-reduce.32.cloned.1.call-update) | async-done | bytes 262160 | tf_op jit(solution)/shard_map/psum | solution.py:25
  609.7 34.4 %all-reduce.34.cloned.1.call-done = f32[512,256]{0,1:T(8,128)} async-done(((f32[512,256]{0,1:T(8,128)}), f32[512,256]{0,1:T(8,128)}) %all-reduce.34.cloned.1.call-update) | async-done | bytes 524304 | tf_op jit(solution)/shard_map/psum | solution.py:110
  644.9 2.5 convolution_bitcast_fusion.14
  647.5 37.4 %all-reduce.36.cloned.1.call-done = f32[512,256]{0,1:T(8,128)} async-done(((f32[512,256]{0,1:T(8,128)}), f32[512,256]{0,1:T(8,128)}) %all-reduce.36.cloned.1.call-update) | async-done | bytes 524304 | tf_op jit(solution)/shard_map/psum | solution.py:110
  687.4 2.5 convolution_bitcast_fusion.13
  690.0 38.4 %all-reduce.38.cloned.1.call-done = f32[512,256]{0,1:T(8,128)} async-done(((f32[512,256]{0,1:T(8,128)}), f32[512,256]{0,1:T(8,128)}) %all-reduce.38.cloned.1.call-update) | async-done | bytes 524304 | tf_op jit(solution)/shard_map/psum | solution.py:110
  729.9 2.7 convolution_bitcast_fusion.12
  732.6 39.8 %all-reduce.40.cloned.1.call-done = f32[512,256]{0,1:T(8,128)} async-done(((f32[512,256]{0,1:T(8,128)}), f32[512,256]{0,1:T(8,128)}) %all-reduce.40.cloned.1.call-update) | async-done | bytes 524304 | tf_op jit(solution)/shard_map/psum | solution.py:110
  774.1 2.7 convolution_bitcast_fusion.11
  776.9 38.8 %all-reduce.42.cloned.1.call-done = f32[512,256]{0,1:T(8,128)} async-done(((f32[512,256]{0,1:T(8,128)}), f32[512,256]{0,1:T(8,128)}) %all-reduce.42.cloned.1.call-update) | async-done | bytes 524304 | tf_op jit(solution)/shard_map/psum | solution.py:110
  817.4 2.7 convolution_bitcast_fusion.10
  820.1 37.4 %all-reduce.44.cloned.1.call-done = f32[512,256]{0,1:T(8,128)} async-done(((f32[512,256]{0,1:T(8,128)}), f32[512,256]{0,1:T(8,128)}) %all-reduce.44.cloned.1.call-update) | async-done | bytes 524304 | tf_op jit(solution)/shard_map/psum | solution.py:110
  859.3 2.7 convolution_bitcast_fusion.9
  862.0 37.4 %all-reduce.46.cloned.1.call-done = f32[512,256]{0,1:T(8,128)} async-done(((f32[512,256]{0,1:T(8,128)}), f32[512,256]{0,1:T(8,128)}) %all-reduce.46.cloned.1.call-update) | async-done | bytes 524304 | tf_op jit(solution)/shard_map/psum | solution.py:110
  899.4 5.6 conditional.30
  901.5 2.4 fusion.64
  906.7 2.7 convolution_bitcast_fusion.8
  909.5 33.3 %all-reduce.48.cloned.1.call-done = f32[512,256]{0,1:T(8,128)} async-done(((f32[512,256]{0,1:T(8,128)}), f32[512,256]{0,1:T(8,128)}) %all-reduce.48.cloned.1.call-update) | async-done | bytes 524304 | tf_op jit(solution)/shard_map/psum | solution.py:110
  942.8 5.6 conditional.31
  950.1 22.7 %all-gather.2.cloned.1.call-done = bf16[4096,256]{1,0:T(8,128)(2,1)} async-done(((bf16[1024,256]{1,0:T(8,128)(2,1)}), bf16[4096,256]{1,0:T(8,128)(2,1)}) %all-gather.2.cloned.1.call-update) | async-done | bytes 2097168 | tf_op jit(solution)/shard_map/all_gather | solution.py:127
  972.9 3.4 collective-permute-start.2
  976.2 3.4 collective-permute-start.3
  979.9 42.9 %collective-permute-done.2 = bf16[4096,256]{1,0:T(8,128)(2,1)} collective-permute-done((bf16[4096,256]{1,0:T(8,128)(2,1)}, bf16[4096,256]{1,0:T(8,128)(2,1)}, u32[]{:S(2)}, u32[]{:S(2)}) %collective-permute-start.2) | collective-permute-done | bytes 2097184 | tf_op jit(solution)/shard_map/ppermute | solution.py:20
  1022.8 44.9 %collective-permute-done.3 = bf16[4096,256]{1,0:T(8,128)(2,1)} collective-permute-done((bf16[4096,256]{1,0:T(8,128)(2,1)}, bf16[4096,256]{1,0:T(8,128)(2,1)}, u32[]{:S(2)}, u32[]{:S(2)}) %collective-permute-start.3) | collective-permute-done | bytes 2097184 | tf_op jit(solution)/shard_map/ppermute | solution.py:20
  1067.8 6.4 pad_maximum_fusion
  1074.2 10.5 reshape.638
  1084.7 4.9 gather_fusion
  1090.7 3.0 fusion.75
  (128 shorter events, 71.3 us)
Async XLA Ops:
  7.2 1.7 copy-start
  7.2 268.0 %reduce-scatter.2.cloned.1.call-start = ((), (), s32[]{:S(2)}) async-start(), calls=%async_computation.1 | async-start | bytes 5242880 | tf_op jit(solution)/shard_map/reduce_scatter | solution.py:70
  10.8 1.0 copy-start.6
  38.6 96.6 %collective-permute-start = (f32[4096,256]{1,0:T(8,128)}, f32[4096,256]{1,0:T(8,128)}, u32[]{:S(2)}, u32[]{:S(2)}) collective-permute-start(f32[4096,256]{1,0:T(8,128)} %squeeze.124), channel_id=1, source_target_pairs={{4,0},{8,4},{12,8},{16,12},{20,16},{24,20},{28,24},{5,1},{9,5},{13... | collective-permute-start | bytes 12582920 | tf_op jit(solution)/shard_map/ppermute | solution.py:20
  46.0 94.2 %collective-permute-start.1 = (f32[4096,256]{1,0:T(8,128)}, f32[4096,256]{1,0:T(8,128)}, u32[]{:S(2)}, u32[]{:S(2)}) collective-permute-start(f32[4096,256]{1,0:T(8,128)} %squeeze.125), channel_id=1, source_target_pairs={{8,0},{12,4},{16,8},{20,12},{24,16},{28,20},{9,1},{13,5},{17,9},{2... | collective-permute-start | bytes 12582920 | tf_op jit(solution)/shard_map/ppermute | solution.py:20
  147.7 130.9 %copy-start.1 = (bf16[1024,512]{1,0:T(8,128)(2,1)S(1)}, bf16[1024,512]{1,0:T(8,128)(2,1)}, u32[]{:S(2)}) copy-start(bf16[1024,512]{1,0:T(8,128)(2,1)} %param.78) | copy-start | bytes 3145732
  147.7 165.5 %all-reduce.18.cloned.1.call-start = ((), (), s32[]{:S(2)}) async-start(), calls=%async_computation.2 | async-start | bytes 524288 | tf_op jit(solution)/shard_map/psum | solution.py:25
  276.7 0.8 copy-start.3
  281.0 74.5 %all-reduce.20.cloned.1.call-start = ((), (), s32[]{:S(2)}) async-start(), calls=%async_computation.3 | async-start | bytes 524288 | tf_op jit(solution)/shard_map/psum | solution.py:25
  323.4 73.1 %all-reduce.22.cloned.1.call-start = ((), (), s32[]{:S(2)}) async-start(), calls=%async_computation.4 | async-start | bytes 524288 | tf_op jit(solution)/shard_map/psum | solution.py:25
  364.4 73.3 %all-reduce.24.cloned.1.call-start = ((), (), s32[]{:S(2)}) async-start(), calls=%async_computation.5 | async-start | bytes 524288 | tf_op jit(solution)/shard_map/psum | solution.py:25
  405.5 74.6 %all-reduce.26.cloned.1.call-start = ((), (), s32[]{:S(2)}) async-start(), calls=%async_computation.6 | async-start | bytes 524288 | tf_op jit(solution)/shard_map/psum | solution.py:25
  446.4 76.1 %all-reduce.28.cloned.1.call-start = ((), (), s32[]{:S(2)}) async-start(), calls=%async_computation.7 | async-start | bytes 524288 | tf_op jit(solution)/shard_map/psum | solution.py:25
  488.8 76.6 %all-reduce.30.cloned.1.call-start = ((), (), s32[]{:S(2)}) async-start(), calls=%async_computation.8 | async-start | bytes 524288 | tf_op jit(solution)/shard_map/psum | solution.py:25
  530.5 41.8 %copy-start.4 = (bf16[512,256]{1,0:T(8,128)(2,1)S(1)}, bf16[512,256]{1,0:T(8,128)(2,1)}, u32[]{:S(2)}) copy-start(bf16[512,256]{1,0:T(8,128)(2,1)} %all-reduce.18.cloned.1.call-done) | copy-start | bytes 786436
  532.0 76.0 %all-reduce.32.cloned.1.call-start = ((), (), s32[]{:S(2)}) async-start(), calls=%async_computation.9 | async-start | bytes 524288 | tf_op jit(solution)/shard_map/psum | solution.py:25
  569.7 74.4 %all-reduce.34.cloned.1.call-start = ((), (), s32[]{:S(2)}) async-start(), calls=%async_computation.10 | async-start | bytes 1048576 | tf_op jit(solution)/shard_map/psum | solution.py:110
  572.3 112.6 %all-reduce.36.cloned.1.call-start = ((), (), s32[]{:S(2)}) async-start(), calls=%async_computation.11 | async-start | bytes 1048576 | tf_op jit(solution)/shard_map/psum | solution.py:110
  644.2 0.7 copy-start.5
  647.4 80.9 %all-reduce.38.cloned.1.call-start = ((), (), s32[]{:S(2)}) async-start(), calls=%async_computation.12 | async-start | bytes 1048576 | tf_op jit(solution)/shard_map/psum | solution.py:110
  686.6 0.8 copy-start.2
  689.9 82.4 %all-reduce.40.cloned.1.call-start = ((), (), s32[]{:S(2)}) async-start(), calls=%async_computation.13 | async-start | bytes 1048576 | tf_op jit(solution)/shard_map/psum | solution.py:110
  732.6 83.1 %all-reduce.42.cloned.1.call-start = ((), (), s32[]{:S(2)}) async-start(), calls=%async_computation.14 | async-start | bytes 1048576 | tf_op jit(solution)/shard_map/psum | solution.py:110
  776.8 80.7 %all-reduce.44.cloned.1.call-start = ((), (), s32[]{:S(2)}) async-start(), calls=%async_computation.15 | async-start | bytes 1048576 | tf_op jit(solution)/shard_map/psum | solution.py:110
  820.1 79.3 %all-reduce.46.cloned.1.call-start = ((), (), s32[]{:S(2)}) async-start(), calls=%async_computation.16 | async-start | bytes 1048576 | tf_op jit(solution)/shard_map/psum | solution.py:110
  862.0 80.8 %all-reduce.48.cloned.1.call-start = ((), (), s32[]{:S(2)}) async-start(), calls=%async_computation.17 | async-start | bytes 1048576 | tf_op jit(solution)/shard_map/psum | solution.py:110
  909.4 63.4 %all-gather.2.cloned.1.call-start = ((), (), s32[]{:S(2)}) async-start(), calls=%async_computation.18 | async-start | bytes 2621440 | tf_op jit(solution)/shard_map/all_gather | solution.py:127
  972.9 50.0 %collective-permute-start.2 = (bf16[4096,256]{1,0:T(8,128)(2,1)}, bf16[4096,256]{1,0:T(8,128)(2,1)}, u32[]{:S(2)}, u32[]{:S(2)}) collective-permute-start(bf16[4096,256]{1,0:T(8,128)(2,1)} %all-gather.2.cloned.1.call-done), channel_id=1, source_target_pairs={{0,4},{4,8},{8,12},{12,16},{16,20},{20,24},{24,28},{1,5},{5,9},{9,... | collective-permute-start | bytes 6291464 | tf_op jit(solution)/shard_map/ppermute | solution.py:20
  976.2 91.5 %collective-permute-start.3 = (bf16[4096,256]{1,0:T(8,128)(2,1)}, bf16[4096,256]{1,0:T(8,128)(2,1)}, u32[]{:S(2)}, u32[]{:S(2)}) collective-permute-start(bf16[4096,256]{1,0:T(8,128)(2,1)} %all-gather.2.cloned.1.call-done), channel_id=1, source_target_pairs={{0,8},{4,12},{8,16},{12,20},{16,24},{20,28},{1,9},{5,13},{9,17},{1... | collective-permute-start | bytes 6291464 | tf_op jit(solution)/shard_map/ppermute | solution.py:20
Sparse Core Ops, SparseCore 0:
  147.8 127.3 reduce-scatter.1
  281.2 31.9 all-reduce.17
  323.5 31.9 all-reduce.19
  364.5 31.9 all-reduce.21
  405.6 31.9 all-reduce.23
  446.5 33.4 all-reduce.25
  489.0 33.4 all-reduce.27
  532.1 33.2 all-reduce.29
  569.8 38.1 all-reduce.31
  610.9 33.1 all-reduce.33
  647.5 37.2 all-reduce.35
  690.1 38.2 all-reduce.37
  732.7 39.6 all-reduce.39
  776.9 38.6 all-reduce.41
  820.2 37.2 all-reduce.43
  862.1 37.2 all-reduce.45
  909.6 33.1 all-reduce.47
  950.2 22.5 all-gather.1
where the time goes:
time: 1100 us
  waiting for transfers between devices  877 us (80%)
  local copies, waits for them, and re-layouts  73.2 us (7%)
  matrix products  63.1 us (6%)
  other arithmetic  61.4 us (6%)
  between operations  14.6 us (1%)
  starting transfers between devices  11.9 us (1%)
    psum x8, waiting for transfers between devices, shards(): summed_later = lax.psum(partial_term, 'sub')  297 us
    psum x8, waiting for transfers between devices, broadcast(): return lax.psum(jnp.where(mine, shard, jnp.zeros_like(shard)), axis)  255 us
    ppermute x4, waiting for transfers between devices, passed_along(): return lax.ppermute(block, axis, route)  175 us
    reduce_scatter x1, waiting for transfers between devices, shards(): lax.psum_scatter(route_forward(spilled), 'sub', scatter_dimension=0, tile...  127 us
    all_gather x1, waiting for transfers between devices, shards(): lax.all_gather(separator_x, 'sub', axis=0, tiled=True)  22.7 us
  transfers between devices with their start and end apart: 22, of which 22 were waited for; matrix products, arithmetic and copies ran while one was open for 2% of the time, Pallas kernels for 0%

commit v1 on v0

v1 whole, which is shorter than its diff:
```python
import functools

import jax
import jax.numpy as jnp
from jax import lax
from jax.experimental import pallas as pl
from jax.experimental.pallas import tpu as pltpu
from jax.sharding import PartitionSpec as P

WSN = 512
SA = 4096
R = 256
BLK = 64
KB = 4
SPAN = 3
MESH = pl.DeviceIdType.MESH
F32 = jnp.float32
BF16 = jnp.bfloat16


def mm(a, b):
    return jnp.dot(a, b, preferred_element_type=F32)


def mm_t(a, b):
    return lax.dot_general(a, b, (((0,), (0,)), ((), ())), preferred_element_type=F32)


def halves(v):
    hi = v.astype(BF16)
    return hi, (v - hi.astype(F32)).astype(BF16)


def kernel(
    S, M,
    right_h, inv_h, panels_h, meta_v, meta_s, sright_h, sinv_h, fac_h,
    ox, osx,
    rt, iv, pn, srt, sinv, fac,
    ly, ub, ucat, usnd, mr, ms,
    accs, accm, pr, ysnd, yrcv, run, yb, runt, xt, trcv, tsnd, xb, pcs, psnd, lo,
    lsem, msem, osem,
    u_ss, u_rs, m_ss, m_rs, p_ss, p_rs, y_ss, y_rs, f_ss, f_rs, t_ss, t_rs,
    xd_ss, xd_rs, xu_ss, xu_rs, b_ss, b_rs,
):
    s = lax.axis_index("leaf")
    m = lax.axis_index("sub")
    c = lax.rem(m, 2)
    y = lax.div(m, 2)
    ny = M // 2
    nl = right_h.shape[0]
    SH = srt.shape[0]
    B = SH // WSN
    nbm = SH // BLK
    c1, c2 = nl - 1, nl - 2
    first = {1: 0, 2: c1}
    base = {1: nl, 2: nl + c1}
    width = {1: c1, 2: c2}
    nslots = nl + c1 + c2
    partner = (s, m + 1 - 2 * c)
    up = (s, m + 1)
    down = (s, m - 1)

    def remote(src, dst, ssem, rsem, dev):
        return pltpu.make_async_remote_copy(
            src_ref=src, dst_ref=dst, send_sem=ssem, recv_sem=rsem, device_id=dev, device_id_type=MESH
        )

    locals_in = [
        (right_h, rt, 0), (inv_h, iv, nl), (panels_h, pn, 2 * nl),
    ]
    for j in range(nl):
        for src, dst, at in locals_in:
            pltpu.make_async_copy(src.at[j], dst.at[j], lsem.at[at + j]).start()
    big = [
        pltpu.make_async_copy(sright_h, srt, lsem.at[3 * nl]),
        pltpu.make_async_copy(sinv_h, sinv, lsem.at[3 * nl + 1]),
        pltpu.make_async_copy(fac_h, fac, lsem.at[3 * nl + 2]),
    ]
    for copy in big:
        copy.start()

    barrier = pltpu.get_barrier_semaphore()

    def greet(dev):
        pl.semaphore_signal(barrier, inc=1, device_id=dev, device_id_type=MESH)

    def when_greet(cond, dev):
        pl.when(cond)(lambda: greet(dev))
        return cond.astype(jnp.int32)

    friends = when_greet(m > 0, down) + when_greet(m < M - 1, up)
    for i in range(1, ny):
        greet((s, lax.rem(y + i, ny) * 2 + c))
    for d in (1, 2):
        friends = friends + when_greet(s >= d, (s - d, m))
        friends = friends + when_greet(s + d < S, (s + d, m))

    @pl.loop(0, nl)
    def _(j):
        for src, dst, at in locals_in:
            pltpu.make_async_copy(src.at[j], dst.at[j], lsem.at[at + j]).wait()
        sol = mm(iv[j], rt[j]).astype(BF16)
        ly[j] = sol
        ub[j] = mm(pn[j], sol).astype(BF16)

    def slots(read, sec):
        dist = [sec - read(j, KB) for j in range(nl)]
        rank = []
        for j in range(nl):
            r = jnp.int32(0)
            for i in range(j):
                r = r + (dist[i] == dist[j]).astype(jnp.int32)
            rank.append(r)
        return dist, rank

    own = lambda j, k: meta_s[j, k]
    dist, rank = slots(own, s)

    pl.semaphore_wait(barrier, friends + (ny - 1))

    def metas(d):
        return remote(meta_v, mr.at[d - 1], m_ss.at[d - 1], m_rs.at[d - 1], (s - d, m))

    def updates(d, third):
        if third:
            a, b = usnd.at[2], ucat.at[2]
            return remote(a, b, u_ss.at[2], u_rs.at[2], (s - d, m))
        a = usnd.at[pl.ds(first[d], 2)]
        b = ucat.at[pl.ds(first[d], 2)]
        return remote(a, b, u_ss.at[d - 1], u_rs.at[d - 1], (s - d, m))

    for d in (2, 1):
        @pl.when(s >= d)
        def _():
            metas(d).start()
            for q in range(width[d]):
                pick = jnp.int32(0)
                for j in range(nl):
                    pick = jnp.where((dist[j] == d) & (rank[j] == q), j, pick)
                usnd[first[d] + q] = ub[pick]
            updates(d, False).start()
    pl.when(s == 1)(lambda: updates(1, True).start())

    for d in (1, 2):
        @pl.when(s + d < S)
        def _():
            metas(d).wait_recv()

        @pl.when(s + d >= S)
        def _():
            mr[d - 1] = jnp.full(mr.shape[1:], -1000, jnp.int32)
            ucat[first[d]:first[d] + 2] = jnp.zeros((2, KB * BLK, R), BF16)

        @pl.when(s < d)
        def _():
            pcs[base[d]:base[d] + 2] = jnp.zeros((2, KB * BLK, R), BF16)
        copy = pltpu.make_async_copy(mr.at[d - 1], ms.at[d - 1], msem.at[d - 1])
        copy.start()
        copy.wait()

    @pl.when(s > 0)
    def _():
        ucat[2] = jnp.zeros((KB * BLK, R), BF16)

    @pl.when(s != 1)
    def _():
        pcs[nl + 2] = jnp.zeros((KB * BLK, R), BF16)

    targets = []
    for j in range(nl):
        targets.append([jnp.where(dist[j] == 0, meta_s[j, k], -1) for k in range(KB)])
    for d in (1, 2):
        read = lambda j, k, d=d: ms[d - 1, j, k]
        rd, rr = slots(read, s + d)
        for q in range(width[d]):
            entry = []
            for k in range(KB):
                t = jnp.int32(-1)
                for j in range(nl):
                    t = jnp.where((rd[j] == d) & (rr[j] == q), read(j, k), t)
                entry.append(t)
            targets.append(entry)

    lane = lax.broadcasted_iota(jnp.int32, (1, KB * BLK), 1)
    rows_of = []
    for entry in targets:
        v = jnp.full((1, KB * BLK), entry[KB - 1] * BLK, jnp.int32)
        for k in range(KB - 1):
            v = jnp.where(lane // BLK == k, entry[k] * BLK, v)
        rows_of.append(v + lane % BLK)

    for d in (1, 2):
        pl.when(s + d < S)(lambda d=d: updates(d, False).wait_recv())
    pl.when(s == 0)(lambda: updates(1, True).wait_recv())

    def scatter(member, put):
        @pl.loop(0, SH // 256)
        def _(i):
            at = member * SH + i * 256
            iota = lax.broadcasted_iota(jnp.int32, (256, KB * BLK), 0) + at
            total = jnp.zeros((256, R), F32)
            for n in range(nslots):
                pick = jnp.where(iota == rows_of[n], 1.0, 0.0).astype(BF16)
                total = total + mm(pick, ub[n] if n < nl else ucat[n - nl])
            put(pl.ds(pl.multiple_of(i * 256, 256), 256), total)

    def pair(at):
        return remote(accs.at[at], pr.at[at], p_ss.at[at], p_rs.at[at], partner)

    def across(to, frm):
        return remote(ysnd.at[to], yrcv.at[frm], y_ss.at[to], y_rs.at[frm], (s, to * 2 + c))

    order = [lax.rem(y + i, ny) for i in range(1, ny)] + [y]
    for o in order:
        def put(rows, total, o=o):
            accs[o, rows, :] = total.astype(BF16)
        scatter(o * 2 + 1 - c, put)
        pair(o).start()
    for n, o in enumerate(order):
        def put(rows, total, o=o):
            accm[o, rows, :] = total
        scatter(o * 2 + c, put)
        pair(o).wait_recv()
        if n < ny - 1:
            ysnd[o] = (accm[o] + pr[o].astype(F32)).astype(BF16)
            across(o, y).start()
    big[0].wait()
    run[...] = srt[...].astype(F32) - accm[y] - pr[y].astype(F32)
    for o in order[:-1]:
        across(o, o).wait_recv()
        run[...] -= yrcv[o].astype(F32)
    run[...] = run[...].astype(BF16).astype(F32)
    big[1].wait()
    big[2].wait()

    def cols(p, q=0, n=None):
        return pl.ds(pl.multiple_of(p * SH + q * WSN, WSN), SH if n is None else n)

    def forward(p):
        return remote(yb.at[p], yb.at[p], f_ss.at[p], f_rs.at[p], up)

    @pl.loop(0, m)
    def _(p):
        forward(p).wait_recv()
        pl.when(m < M - 1)(lambda: forward(p).start())
        for b in range(B):
            at = pl.ds(b * WSN, WSN)
            run[at, :] -= mm(fac[at, cols(p)], yb[p])

    for b in range(B):
        at = pl.ds(b * WSN, WSN)
        bracket = run[at, :]
        for e in range(b):
            bracket = bracket - mm(fac[at, cols(m, e, WSN)], yb[m, pl.ds(e * WSN, WSN), :])
        hi, low = halves(bracket)
        block = (mm(sinv[at, :], hi) + mm(sinv[at, :], low)).astype(BF16)
        yb[m, at, :] = block
    pl.when(m < M - 1)(lambda: forward(m).start())
    for b in range(B):
        at = pl.ds(b * WSN, WSN)
        runt[:, at] = yb[m, at, :].astype(F32).T

    def back(p):
        return remote(tsnd.at[p], trcv.at[p], t_ss.at[p], t_rs.at[p], down)

    @pl.when(m < M - 1)
    def _():
        back(m).wait_recv()
        runt[...] -= trcv[m].astype(F32)

    for b in reversed(range(B)):
        at = pl.ds(b * WSN, WSN)
        bracket = runt[:, at]
        for e in range(b + 1, B):
            rows = pl.ds(e * WSN, WSN)
            bracket = bracket - mm(xt[:, rows], fac[rows, cols(m, b, WSN)])
        hi, low = halves(bracket)
        xt[:, at] = (mm(hi, sinv[at, :]) + mm(low, sinv[at, :])).astype(BF16)

    @pl.loop(0, m)
    def _(i):
        p = m - 1 - i
        pl.when(m < M - 1)(lambda: back(p).wait_recv())
        for b in range(B):
            at = pl.ds(b * WSN, WSN)
            term = mm(xt[...], fac[:, cols(p, b, WSN)])
            before = jnp.where(m < M - 1, trcv[p, :, at].astype(F32), 0.0)
            tsnd[p, :, at] = (term + before).astype(BF16)
        back(p).start()

    for b in range(B):
        block = xt[:, b * WSN:(b + 1) * WSN].astype(F32).T.astype(BF16)
        xb[pl.ds(m * nbm + b * (WSN // BLK), WSN // BLK)] = block.reshape(WSN // BLK, BLK, R)

    def xdown(p):
        part = xb.at[pl.ds(p * nbm, nbm)]
        return remote(part, part, xd_ss.at[p], xd_rs.at[p], down)

    def xup(p):
        part = xb.at[pl.ds(p * nbm, nbm)]
        return remote(part, part, xu_ss.at[p], xu_rs.at[p], up)

    pl.when(m < M - 1)(lambda: xup(m).start())
    pl.when(m > 0)(lambda: xdown(m).start())
    out_sep = pltpu.make_async_copy(xb.at[pl.ds(m * nbm, nbm)], osx, osem.at[nl])
    out_sep.start()

    @pl.loop(m + 1, M)
    def _(p):
        xdown(p).wait_recv()
        pl.when(m > 0)(lambda: xdown(p).start())

    @pl.loop(0, m)
    def _(i):
        p = m - 1 - i
        xup(p).wait_recv()
        pl.when(m < M - 1)(lambda: xup(p).start())

    def pieces(d, third):
        if third:
            return remote(psnd.at[2], pcs.at[nl + 2], b_ss.at[2], b_rs.at[2], (s + d, m))
        a = psnd.at[pl.ds(first[d], 2)]
        b = pcs.at[pl.ds(base[d], 2)]
        return remote(a, b, b_ss.at[d - 1], b_rs.at[d - 1], (s + d, m))

    for d in (2, 1):
        @pl.when(s + d < S)
        def _():
            for q in range(width[d]):
                for k in range(KB):
                    t = jnp.maximum(targets[base[d] + q][k], 0)
                    psnd[first[d] + q, k * BLK:(k + 1) * BLK, :] = xb[t]
            pieces(d, False).start()
    pl.when(s == 0)(lambda: pieces(1, True).start())
    for j in range(nl):
        for k in range(KB):
            pcs[j, k * BLK:(k + 1) * BLK, :] = xb[meta_s[j, k]]
    for d in (1, 2):
        pl.when(s >= d)(lambda d=d: pieces(d, False).wait_recv())
    pl.when(s == 1)(lambda: pieces(1, True).wait_recv())

    for j in range(nl):
        at = jnp.where(dist[j] == 0, j, jnp.where(dist[j] == 1, nl + rank[j], nl + c1 + rank[j]))
        at = jnp.clip(at, 0, nslots - 1)
        reduced = mm_t(pn[j], pcs[at])
        inner = (ly[j].astype(F32) - reduced).astype(BF16)
        lo[j] = mm_t(iv[j], inner).astype(BF16)
        pltpu.make_async_copy(lo.at[j], ox.at[j], osem.at[j]).start()

    for d in (1, 2):
        @pl.when(s >= d)
        def _():
            metas(d).wait_send()
            updates(d, False).wait_send()

        pl.when(s + d < S)(lambda d=d: pieces(d, False).wait_send())
    pl.when(s == 1)(lambda: updates(1, True).wait_send())
    pl.when(s == 0)(lambda: pieces(1, True).wait_send())
    for o in order:
        pair(o).wait_send()
    for o in order[:-1]:
        across(o, y).wait_send()

    @pl.when(m < M - 1)
    def _():
        @pl.loop(0, m + 1)
        def _(p):
            forward(p).wait_send()
            xup(p).wait_send()

    @pl.when(m > 0)
    def _():
        @pl.loop(0, m)
        def _(p):
            back(p).wait_send()

        @pl.loop(m, M)
        def _(p):
            xdown(p).wait_send()

    out_sep.wait()
    for j in range(nl):
        pltpu.make_async_copy(lo.at[j], ox.at[j], osem.at[j]).wait()


def shards(S, M, leaf_right, leaf_inverse, panels, leaf_subtree, panel_block, separator_right, separator_inverse, separator_factor):
    nl, W = leaf_right.shape[:2]
    SH = separator_right.shape[0]
    ny = M // 2
    nbm = SH // BLK
    nslots = 3 * nl - 3
    meta = jnp.concatenate([panel_block, leaf_subtree[:, None]], axis=1)
    meta = jnp.pad(meta, ((0, 8 - nl), (0, 128 - KB - 1)))
    anywhere = pl.BlockSpec(memory_space=pl.ANY)
    V = pltpu.VMEM
    D = pltpu.SemaphoreType.DMA
    scratch = [
        V((nl, W, R), BF16), V((nl, W, W), BF16), V((nl, KB * BLK, W), BF16),
        V((SH, R), BF16), V((SH, WSN), BF16), V((SH, SA), BF16),
        V((nl, W, R), BF16), V((nl, KB * BLK, R), BF16), V((2 * nl - 3, KB * BLK, R), BF16), V((2 * nl - 3, KB * BLK, R), BF16),
        V((2, 8, 128), jnp.int32), pltpu.SMEM((2, 8, 128), jnp.int32),
        V((ny, SH, R), BF16), V((ny, SH, R), F32), V((ny, SH, R), BF16), V((ny, SH, R), BF16), V((ny, SH, R), BF16),
        V((SH, R), F32), V((M, SH, R), BF16), V((R, SH), F32), V((R, SH), BF16),
        V((M, R, SH), BF16), V((M, R, SH), BF16), V((SA // BLK, BLK, R), BF16),
        V((nslots, KB * BLK, R), BF16), V((2 * nl - 3, KB * BLK, R), BF16), V((nl, W, R), BF16),
        D((3 * nl + 3,)), D((2,)), D((nl + 1,)),
        D((3,)), D((3,)), D((2,)), D((2,)), D((ny,)), D((ny,)), D((ny,)), D((ny,)),
        D((M,)), D((M,)), D((M,)), D((M,)), D((M,)), D((M,)), D((M,)), D((M,)), D((3,)), D((3,)),
    ]
    leaf_x, sep_x = pl.pallas_call(
        functools.partial(kernel, S, M),
        out_shape=(
            jax.ShapeDtypeStruct((nl, W, R), BF16),
            jax.ShapeDtypeStruct((nbm, BLK, R), BF16),
        ),
        in_specs=[
            anywhere, anywhere, anywhere,
            pl.BlockSpec(memory_space=pltpu.VMEM), pl.BlockSpec(memory_space=pltpu.SMEM),
            anywhere, anywhere, anywhere,
        ],
        out_specs=(anywhere, anywhere),
        scratch_shapes=scratch,
        compiler_params=pltpu.CompilerParams(
            collective_id=0, has_side_effects=True, vmem_limit_bytes=56 * 1024 * 1024
        ),
        cost_estimate=pl.CostEstimate(flops=12_000_000_000, bytes_accessed=16_000_000, transcendentals=0),
    )(leaf_right, leaf_inverse, panels, meta, meta, separator_right, separator_inverse, separator_factor)
    return leaf_x, sep_x.reshape(SH, R)


def solution(mesh):
    placed = (
        P(("leaf", "sub"), None, None),
        P(("leaf", "sub"), None, None),
        P(("leaf", "sub"), None, None),
        P(("leaf", "sub")),
        P(("leaf", "sub"), None),
        P(("leaf", "sub"), None),
        P(("leaf", "sub"), None),
        P(("leaf", "sub"), None),
    )
    return jax.shard_map(
        functools.partial(shards, mesh.shape["leaf"], mesh.shape["sub"]),
        mesh=mesh,
        in_specs=placed,
        out_specs=(P(("leaf", "sub"), None, None), P(("leaf", "sub"), None)),
        check_vma=False,
    )
```

time: 1100 us -> 122 us (0.11)
  the two profiles are of different devices: /device:TPU:10 before, /device:TPU:13 now
where the time goes in v1:
time: 122 us; the launch traced here: 121 us
  Pallas kernels  114 us (93%)
  local copies, waits for them, and re-layouts  5.47 us (4%)
    pallas_call x1, Pallas kernels, shards(): pl.pallas_call(functools.partial(kernel, S, M), out_shape=(jax.ShapeDtype...  114 us
    unnamed x2, local copies, waits for them, and re-layouts  4.13 us

profile of v1, /device:TPU:13, one launch (start us, length us, event | category | flops | bytes accessed | tf_op | source)
XLA Modules:
  0.0 121.2 jit_solution(7604648857813301835)
XLA Ops:
  0.6 0.7 copy.10
  1.4 0.8 pad_add_fusion
  2.1 0.6 pad.4.meta_v.meta_s
  2.7 114.3 %shard_map.95 = (bf16[4,512,256]{2,1,0:T(8,128)(2,1)}, bf16[16,64,256]{2,1,0:T(8,128)(2,1)}) custom-call(bf16[4,512,256]{2,1,0:T(8,128)(2,1)} %right_h.1, bf16[4,512,512]{2,1,0:T(8,128)(2,1)} %inv_h.1, bf16[4,256,512]{2,1,0:T(8,128)(2,1)} %panels_h.1, s32[8,128]{1,0:T(8,128)} %pad.4.meta_v.meta_s, s32[8,128]{1,0:T(8,128)} %pad.4.meta_v.meta_s, ...), custom_call_target="tpu_custom_call" | custom-call | flops 12000000000 | bytes 16000000 | tf_op jit(solution)/shard_map/pallas_call | solution.py:410
  117.0 2.3 %copy.13 = bf16[4,512,256]{2,1,0:T(8,128)(2,1)} copy(bf16[4,512,256]{2,1,0:T(8,128)(2,1)} %get-tuple-element.8) | data formatting | bytes 2097152
  119.3 1.9 %copy.14 = bf16[1024,256]{1,0:T(8,128)(2,1)} copy(bf16[1024,256]{1,0:T(8,128)(2,1)} %bitcast.2) | data formatting | bytes 1048576

commit v2 on v1

v2 whole, which is shorter than its diff:
```python
import functools

import jax
import jax.numpy as jnp
from jax import lax
from jax.experimental import pallas as pl
from jax.experimental.pallas import tpu as pltpu
from jax.sharding import PartitionSpec as P

WSN = 512
SA = 4096
R = 256
BLK = 64
KB = 4
SPAN = 3
MESH = pl.DeviceIdType.MESH
F32 = jnp.float32
BF16 = jnp.bfloat16


def mm(a, b):
    return jnp.dot(a, b, preferred_element_type=F32)


def mm_t(a, b):
    return lax.dot_general(a, b, (((0,), (0,)), ((), ())), preferred_element_type=F32)


def halves(v):
    hi = v.astype(BF16)
    return hi, (v - hi.astype(F32)).astype(BF16)


def kernel(
    S, M,
    right_h, inv_h, panels_h, block_s, tree_s, sright_h, sinv_h, fac_h,
    ox, osx,
    rt, iv, pn, srt, sinv, fac,
    ivt, pnt, ly, ub, ucat, usnd, mv, mr, ms,
    accm, accs, pr, ysnd, yrcv, run, yb, runt, xt, trcv, tsnd, xb, pcs, psnd, lo,
    lsem, msem, osem,
    u_ss, u_rs, m_ss, m_rs, p_ss, p_rs, y_ss, y_rs, f_ss, f_rs, t_ss, t_rs,
    xd_ss, xd_rs, xu_ss, xu_rs, b_ss, b_rs,
):
    s = lax.axis_index("leaf")
    m = lax.axis_index("sub")
    c = lax.rem(m, 2)
    y = lax.div(m, 2)
    ny = M // 2
    nl = right_h.shape[0]
    SH = srt.shape[0]
    B = SH // WSN
    nbm = SH // BLK
    c1, c2 = nl - 1, nl - 2
    first = {1: 0, 2: c1}
    base = {1: nl, 2: nl + c1}
    width = {1: c1, 2: c2}
    nslots = nl + c1 + c2
    partner = (s, m + 1 - 2 * c)
    up = (s, m + 1)
    down = (s, m - 1)

    def remote(src, dst, ssem, rsem, dev):
        return pltpu.make_async_remote_copy(
            src_ref=src, dst_ref=dst, send_sem=ssem, recv_sem=rsem, device_id=dev, device_id_type=MESH
        )

    locals_in = [
        (right_h, rt, 0), (inv_h, iv, nl), (panels_h, pn, 2 * nl),
    ]
    for j in range(nl):
        for src, dst, at in locals_in:
            pltpu.make_async_copy(src.at[j], dst.at[j], lsem.at[at + j]).start()
    big = [
        pltpu.make_async_copy(sright_h, srt, lsem.at[3 * nl]),
        pltpu.make_async_copy(sinv_h, sinv, lsem.at[3 * nl + 1]),
        pltpu.make_async_copy(fac_h, fac, lsem.at[3 * nl + 2]),
    ]
    for copy in big:
        copy.start()

    barrier = pltpu.get_barrier_semaphore()

    def greet(dev):
        pl.semaphore_signal(barrier, inc=1, device_id=dev, device_id_type=MESH)

    def when_greet(cond, dev):
        pl.when(cond)(lambda: greet(dev))
        return cond.astype(jnp.int32)

    friends = when_greet(m > 0, down) + when_greet(m < M - 1, up)
    for i in range(1, ny):
        greet((s, lax.rem(y + i, ny) * 2 + c))
    for d in (1, 2):
        friends = friends + when_greet(s >= d, (s - d, m))
        friends = friends + when_greet(s + d < S, (s + d, m))

    @pl.loop(0, nl)
    def _(j):
        for src, dst, at in locals_in:
            pltpu.make_async_copy(src.at[j], dst.at[j], lsem.at[at + j]).wait()
        sol = mm(iv[j], rt[j]).astype(BF16)
        ly[j] = sol
        ub[j] = mm(pn[j], sol).astype(BF16)

    def slots(read, sec):
        dist = [sec - read(j, KB) for j in range(nl)]
        rank = []
        for j in range(nl):
            r = jnp.int32(0)
            for i in range(j):
                r = r + (dist[i] == dist[j]).astype(jnp.int32)
            rank.append(r)
        return dist, rank

    own = lambda j, k: tree_s[j] if k == KB else block_s[j, k]
    sub = lax.broadcasted_iota(jnp.int32, mv.shape, 0)
    lane = lax.broadcasted_iota(jnp.int32, mv.shape, 1)
    meta = jnp.zeros(mv.shape, jnp.int32)
    for j in range(nl):
        for k in range(KB + 1):
            meta = jnp.where((sub == j) & (lane == k), own(j, k), meta)
    mv[...] = meta
    dist, rank = slots(own, s)

    pl.semaphore_wait(barrier, friends + (ny - 1))

    def metas(d):
        return remote(mv, mr.at[d - 1], m_ss.at[d - 1], m_rs.at[d - 1], (s - d, m))

    def updates(d, third):
        if third:
            a, b = usnd.at[2], ucat.at[2]
            return remote(a, b, u_ss.at[2], u_rs.at[2], (s - d, m))
        a = usnd.at[pl.ds(first[d], 2)]
        b = ucat.at[pl.ds(first[d], 2)]
        return remote(a, b, u_ss.at[d - 1], u_rs.at[d - 1], (s - d, m))

    for d in (2, 1):
        @pl.when(s >= d)
        def _():
            metas(d).start()
            for q in range(width[d]):
                pick = jnp.int32(0)
                for j in range(nl):
                    pick = jnp.where((dist[j] == d) & (rank[j] == q), j, pick)
                usnd[first[d] + q] = ub[pick]
            updates(d, False).start()
    pl.when(s == 1)(lambda: updates(1, True).start())

    def row_ids(entry):
        lane = lax.broadcasted_iota(jnp.int32, (1, KB * BLK), 1)
        v = jnp.full((1, KB * BLK), entry[KB - 1] * BLK, jnp.int32)
        for k in range(KB - 1):
            v = jnp.where(lane // BLK == k, entry[k] * BLK, v)
        return v + lane % BLK

    def scatter(begin, blocks, pairs, put):
        @pl.loop(0, blocks)
        def _(i):
            at = begin + i * 256
            iota = lax.broadcasted_iota(jnp.int32, (256, KB * BLK), 0) + at
            total = jnp.zeros((256, R), F32)
            for ids, ref, n in pairs:
                pick = jnp.where(iota == ids, 1.0, 0.0).astype(BF16)
                total = total + mm(pick, ref[n])
            put(pl.ds(pl.multiple_of(at, 256), 256), total)

    targets = []
    for j in range(nl):
        targets.append([jnp.where(dist[j] == 0, block_s[j, k], -1) for k in range(KB)])
    pairs = [(row_ids(targets[j]), ub, j) for j in range(nl)]

    def put_own(rows, total):
        accm[rows, :] = total
    scatter(0, SA // 256, pairs, put_own)

    @pl.loop(0, nl)
    def _(j):
        ivt[j] = iv[j].astype(F32).T.astype(BF16)
        pnt[j] = pn[j].astype(F32).T.astype(BF16)

    for d in (1, 2):
        @pl.when(s + d < S)
        def _():
            metas(d).wait_recv()

        @pl.when(s + d >= S)
        def _():
            mr[d - 1] = jnp.full(mr.shape[1:], -1000, jnp.int32)
            ucat[first[d]:first[d] + 2] = jnp.zeros((2, KB * BLK, R), BF16)

        @pl.when(s < d)
        def _():
            pcs[base[d]:base[d] + 2] = jnp.zeros((2, KB * BLK, R), BF16)
        copy = pltpu.make_async_copy(mr.at[d - 1], ms.at[d - 1], msem.at[d - 1])
        copy.start()
        copy.wait()

    @pl.when(s > 0)
    def _():
        ucat[2] = jnp.zeros((KB * BLK, R), BF16)

    @pl.when(s != 1)
    def _():
        pcs[nl + 2] = jnp.zeros((KB * BLK, R), BF16)

    pairs = []
    for d in (1, 2):
        read = lambda j, k, d=d: ms[d - 1, j, k]
        rd, rr = slots(read, s + d)
        for q in range(width[d]):
            entry = []
            for k in range(KB):
                t = jnp.int32(-1)
                for j in range(nl):
                    t = jnp.where((rd[j] == d) & (rr[j] == q), read(j, k), t)
                entry.append(t)
            targets.append(entry)
            pairs.append((row_ids(entry), ucat, first[d] + q))
    third = pairs.pop(2)

    for d in (1, 2):
        pl.when(s + d < S)(lambda d=d: updates(d, False).wait_recv())

    def put_more(rows, total):
        accm[rows, :] += total

    @pl.when(s == 0)
    def _():
        updates(1, True).wait_recv()
        scatter(0, SA // 256, [third], put_more)

    def pair(o, b):
        return remote(accs.at[o, b], pr.at[o, b], p_ss.at[o, b], p_rs.at[o, b], partner)

    def across(to, frm, b):
        return remote(ysnd.at[to, b], yrcv.at[frm, b], y_ss.at[to, b], y_rs.at[frm, b], (s, to * 2 + c))

    def rows_at(o, core, b):
        return pl.ds(pl.multiple_of((o * 2 + core) * SH + b * WSN, WSN), WSN)

    def more(o, core, b):
        scatter((o * 2 + core) * SH + b * WSN, WSN // 256, pairs, put_more)

    order = [lax.rem(y + i, ny) for i in range(1, ny)] + [y]
    for o in order:
        for b in range(B):
            more(o, 1 - c, b)
            accs[o, b] = accm[rows_at(o, 1 - c, b), :].astype(BF16)
            pair(o, b).start()
        for b in range(B):
            more(o, c, b)
            if o is not y:
                pair(o, b).wait_recv()
                ysnd[o, b] = (accm[rows_at(o, c, b), :] + pr[o, b].astype(F32)).astype(BF16)
                across(o, y, b).start()
    big[0].wait()
    big[1].wait()
    big[2].wait()

    def right_side(b):
        at = pl.ds(b * WSN, WSN)
        pair(y, b).wait_recv()
        side = srt[at, :].astype(F32) - accm[rows_at(y, c, b), :] - pr[y, b].astype(F32)
        for o in order[:-1]:
            across(o, o, b).wait_recv()
            side = side - yrcv[o, b].astype(F32)
        run[at, :] = side.astype(BF16).astype(F32)

    def cols(q):
        return pl.ds(pl.multiple_of(q * WSN, WSN), WSN)

    def forward(q):
        return remote(yb.at[q], yb.at[q], f_ss.at[q], f_rs.at[q], up)

    @pl.when(m > 0)
    def _():
        for b in range(B):
            right_side(b)

    @pl.loop(0, m * B)
    def _(q):
        forward(q).wait_recv()
        pl.when(m < M - 1)(lambda: forward(q).start())
        for b in range(B):
            at = pl.ds(b * WSN, WSN)
            run[at, :] -= mm(fac[at, cols(q)], yb[q])

    for b in range(B):
        at = pl.ds(b * WSN, WSN)
        pl.when(m == 0)(lambda b=b: right_side(b))
        bracket = run[at, :]
        for e in range(b):
            bracket = bracket - mm(fac[at, cols(m * B + e)], yb[m * B + e])
        hi, low = halves(bracket)
        yb[m * B + b] = (mm(sinv[at, :], hi) + mm(sinv[at, :], low)).astype(BF16)
        pl.when(m < M - 1)(lambda b=b: forward(m * B + b).start())
    for b in range(B):
        runt[:, b * WSN:(b + 1) * WSN] = yb[m * B + b].astype(F32).T

    def back(q):
        return remote(tsnd.at[q], trcv.at[q], t_ss.at[q], t_rs.at[q], down)

    nbs = WSN // BLK

    def xdown(q):
        part = xb.at[pl.ds(q * nbs, nbs)]
        return remote(part, part, xd_ss.at[q], xd_rs.at[q], down)

    def xup(q):
        part = xb.at[pl.ds(q * nbs, nbs)]
        return remote(part, part, xu_ss.at[q], xu_rs.at[q], up)

    def send_x(b):
        block = xt[:, b * WSN:(b + 1) * WSN].astype(F32).T.astype(BF16)
        q = m * B + b
        xb[pl.ds(q * nbs, nbs)] = block.reshape(nbs, BLK, R)
        pl.when(m < M - 1)(lambda: xup(q).start())
        pl.when(m > 0)(lambda: xdown(q).start())

    for b in reversed(range(B)):
        at = pl.ds(b * WSN, WSN)

        @pl.when(m < M - 1)
        def _():
            back(m * B + b).wait_recv()
            runt[:, at] -= trcv[m * B + b].astype(F32)
        bracket = runt[:, at]
        for e in range(b + 1, B):
            rows = pl.ds(e * WSN, WSN)
            bracket = bracket - mm(xt[:, rows], fac[rows, cols(m * B + b)])
        hi, low = halves(bracket)
        xt[:, at] = (mm(hi, sinv[at, :]) + mm(low, sinv[at, :])).astype(BF16)
        pl.when(m == 0)(lambda b=b: send_x(b))

    @pl.loop(0, m * B)
    def _(i):
        q = m * B - 1 - i
        pl.when(m < M - 1)(lambda: back(q).wait_recv())
        term = mm(xt[...], fac[:, cols(q)])
        before = jnp.where(m < M - 1, trcv[q].astype(F32), 0.0)
        tsnd[q] = (term + before).astype(BF16)
        back(q).start()

    @pl.when(m > 0)
    def _():
        @pl.loop(0, m * B)
        def _(q):
            back(q).wait_send()
        for b in reversed(range(B)):
            send_x(b)

    out_sep = pltpu.make_async_copy(xb.at[pl.ds(m * nbm, nbm)], osx, osem.at[nl])
    out_sep.start()

    @pl.loop(0, (M - 1 - m) * B)
    def _(i):
        q = M * B - 1 - i
        xdown(q).wait_recv()
        pl.when(m > 0)(lambda: xdown(q).start())

    @pl.loop(0, m * B)
    def _(i):
        q = m * B - 1 - i
        xup(q).wait_recv()
        pl.when(m < M - 1)(lambda: xup(q).start())

    def pieces(d, third):
        if third:
            return remote(psnd.at[2], pcs.at[nl + 2], b_ss.at[2], b_rs.at[2], (s + d, m))
        a = psnd.at[pl.ds(first[d], 2)]
        b = pcs.at[pl.ds(base[d], 2)]
        return remote(a, b, b_ss.at[d - 1], b_rs.at[d - 1], (s + d, m))

    for d in (2, 1):
        @pl.when(s + d < S)
        def _():
            for q in range(width[d]):
                for k in range(KB):
                    t = jnp.maximum(targets[base[d] + q][k], 0)
                    psnd[first[d] + q, k * BLK:(k + 1) * BLK, :] = xb[t]
            pieces(d, False).start()
    pl.when(s == 0)(lambda: pieces(1, True).start())
    for j in range(nl):
        for k in range(KB):
            pcs[j, k * BLK:(k + 1) * BLK, :] = xb[block_s[j, k]]
    for d in (1, 2):
        pl.when(s >= d)(lambda d=d: pieces(d, False).wait_recv())
    pl.when(s == 1)(lambda: pieces(1, True).wait_recv())

    for j in range(nl):
        at = jnp.where(dist[j] == 0, j, jnp.where(dist[j] == 1, nl + rank[j], nl + c1 + rank[j]))
        at = jnp.clip(at, 0, nslots - 1)
        reduced = mm(pnt[j], pcs[at])
        inner = (ly[j].astype(F32) - reduced).astype(BF16)
        lo[j] = mm(ivt[j], inner).astype(BF16)
        pltpu.make_async_copy(lo.at[j], ox.at[j], osem.at[j]).start()

    for d in (1, 2):
        @pl.when(s >= d)
        def _():
            metas(d).wait_send()
            updates(d, False).wait_send()

        pl.when(s + d < S)(lambda d=d: pieces(d, False).wait_send())
    pl.when(s == 1)(lambda: updates(1, True).wait_send())
    pl.when(s == 0)(lambda: pieces(1, True).wait_send())
    for o in order:
        for b in range(B):
            pair(o, b).wait_send()
            if o is not y:
                across(o, y, b).wait_send()

    @pl.when(m < M - 1)
    def _():
        @pl.loop(0, (m + 1) * B)
        def _(q):
            forward(q).wait_send()
            xup(q).wait_send()

    @pl.when(m > 0)
    def _():
        @pl.loop(m * B, M * B)
        def _(q):
            xdown(q).wait_send()

    out_sep.wait()
    for j in range(nl):
        pltpu.make_async_copy(lo.at[j], ox.at[j], osem.at[j]).wait()


def shards(S, M, leaf_right, leaf_inverse, panels, leaf_subtree, panel_block, separator_right, separator_inverse, separator_factor):
    nl, W = leaf_right.shape[:2]
    SH = separator_right.shape[0]
    ny = M // 2
    nbm = SH // BLK
    B = SH // WSN
    N = SA // WSN
    nslots = 3 * nl - 3
    anywhere = pl.BlockSpec(memory_space=pl.ANY)
    V = pltpu.VMEM
    D = pltpu.SemaphoreType.DMA
    scratch = [
        V((nl, W, R), BF16), V((nl, W, W), BF16), V((nl, KB * BLK, W), BF16),
        V((SH, R), BF16), V((SH, WSN), BF16), V((SH, SA), BF16),
        V((nl, W, W), BF16), V((nl, W, KB * BLK), BF16),
        V((nl, W, R), BF16), V((nl, KB * BLK, R), BF16), V((2 * nl - 3, KB * BLK, R), BF16), V((2 * nl - 3, KB * BLK, R), BF16),
        V((8, 128), jnp.int32), V((2, 8, 128), jnp.int32), pltpu.SMEM((2, 8, 128), jnp.int32),
        V((SA, R), F32), V((ny, B, WSN, R), BF16), V((ny, B, WSN, R), BF16), V((ny, B, WSN, R), BF16), V((ny, B, WSN, R), BF16),
        V((SH, R), F32), V((N, WSN, R), BF16), V((R, SH), F32), V((R, SH), BF16),
        V((N, R, WSN), BF16), V((N, R, WSN), BF16), V((SA // BLK, BLK, R), BF16),
        V((nslots, KB * BLK, R), BF16), V((2 * nl - 3, KB * BLK, R), BF16), V((nl, W, R), BF16),
        D((3 * nl + 3,)), D((2,)), D((nl + 1,)),
        D((3,)), D((3,)), D((2,)), D((2,)), D((ny, B)), D((ny, B)), D((ny, B)), D((ny, B)),
        D((N,)), D((N,)), D((N,)), D((N,)), D((N,)), D((N,)), D((N,)), D((N,)), D((3,)), D((3,)),
    ]
    leaf_x, sep_x = pl.pallas_call(
        functools.partial(kernel, S, M),
        out_shape=(
            jax.ShapeDtypeStruct((nl, W, R), BF16),
            jax.ShapeDtypeStruct((nbm, BLK, R), BF16),
        ),
        in_specs=[
            anywhere, anywhere, anywhere,
            pl.BlockSpec(memory_space=pltpu.SMEM), pl.BlockSpec(memory_space=pltpu.SMEM),
            anywhere, anywhere, anywhere,
        ],
        out_specs=(anywhere, anywhere),
        scratch_shapes=scratch,
        compiler_params=pltpu.CompilerParams(
            collective_id=0, has_side_effects=True, vmem_limit_bytes=56 * 1024 * 1024
        ),
        cost_estimate=pl.CostEstimate(flops=12_000_000_000, bytes_accessed=16_000_000, transcendentals=0),
    )(leaf_right, leaf_inverse, panels, panel_block, leaf_subtree, separator_right, separator_inverse, separator_factor)
    return leaf_x, sep_x.reshape(SH, R)


def solution(mesh):
    placed = (
        P(("leaf", "sub"), None, None),
        P(("leaf", "sub"), None, None),
        P(("leaf", "sub"), None, None),
        P(("leaf", "sub")),
        P(("leaf", "sub"), None),
        P(("leaf", "sub"), None),
        P(("leaf", "sub"), None),
        P(("leaf", "sub"), None),
    )
    return jax.shard_map(
        functools.partial(shards, mesh.shape["leaf"], mesh.shape["sub"]),
        mesh=mesh,
        in_specs=placed,
        out_specs=(P(("leaf", "sub"), None, None), P(("leaf", "sub"), None)),
        check_vma=False,
    )
```

time: 122 us -> 113 us (0.926)
  Pallas kernels: 114 us -> 108 us
  local copies, waits for them, and re-layouts: 5.47 us -> 4.13 us
    pallas_call x1, Pallas kernels: 114 us -> 108 us  [shards(): pl.pallas_call(functools.partial(kernel, S, M), out_shape=(jax.ShapeDtype...]
where the time goes in v2:
time: 113 us; the launch traced here: 112 us
  Pallas kernels  108 us (96%)
  local copies, waits for them, and re-layouts  4.13 us (4%)
    pallas_call x1, Pallas kernels, shards(): pl.pallas_call(functools.partial(kernel, S, M), out_shape=(jax.ShapeDtype...  108 us
    unnamed x2, local copies, waits for them, and re-layouts  4.13 us

profile of v2, /device:TPU:13, one launch (start us, length us, event | category | flops | bytes accessed | tf_op | source)
XLA Modules:
  0.0 112.4 jit_solution(1647880050444756298)
XLA Ops:
  0.6 107.6 %shard_map.95 = (bf16[4,512,256]{2,1,0:T(8,128)(2,1)}, bf16[16,64,256]{2,1,0:T(8,128)(2,1)}) custom-call(bf16[4,512,256]{2,1,0:T(8,128)(2,1)} %right_h.1, bf16[4,512,512]{2,1,0:T(8,128)(2,1)} %inv_h.1, bf16[4,256,512]{2,1,0:T(8,128)(2,1)} %panels_h.1, s32[4,4]{1,0:T(4,128)} %block_s.1, s32[4]{0:T(128)} %tree_s.1, bf16[1024,256]{1,0:T(8,128)(2,1)} %sright_h.1, ...), custom_call_target="tpu_custom_call" | custom-call | flops 12000000000 | bytes 16000000 | tf_op jit(solution)/shard_map/pallas_call | solution.py:458
  108.3 2.3 %copy.12 = bf16[4,512,256]{2,1,0:T(8,128)(2,1)} copy(bf16[4,512,256]{2,1,0:T(8,128)(2,1)} %get-tuple-element.8) | data formatting | bytes 2097152
  110.5 1.9 %copy.13 = bf16[1024,256]{1,0:T(8,128)(2,1)} copy(bf16[1024,256]{1,0:T(8,128)(2,1)} %bitcast.1) | data formatting | bytes 1048576

commit v3 on v2

--- a/solution.py
+++ b/solution.py
@@ -24,11 +24,6 @@
 
 def mm_t(a, b):
     return lax.dot_general(a, b, (((0,), (0,)), ((), ())), preferred_element_type=F32)
-
-
-def halves(v):
-    hi = v.astype(BF16)
-    return hi, (v - hi.astype(F32)).astype(BF16)
 
 
 def kernel(
@@ -220,9 +215,6 @@
             pairs.append((row_ids(entry), ucat, first[d] + q))
     third = pairs.pop(2)
 
-    for d in (1, 2):
-        pl.when(s + d < S)(lambda d=d: updates(d, False).wait_recv())
-
     def put_more(rows, total):
         accm[rows, :] += total
 
@@ -230,6 +222,27 @@
     def _():
         updates(1, True).wait_recv()
         scatter(0, SA // 256, [third], put_more)
+
+    even = lax.rem(s, 2) == 0
+    near, far = pairs[:2], pairs[2:]
+
+    def arrived(d):
+        pl.when(s + d < S)(lambda: updates(d, False).wait_recv())
+
+    @pl.when(even)
+    def _():
+        arrived(1)
+        scatter(0, SA // 256, near, put_more)
+        arrived(2)
+
+    @pl.when(jnp.logical_not(even))
+    def _():
+        arrived(2)
+        scatter(0, SA // 256, far, put_more)
+        arrived(1)
+    pairs = [
+        (jnp.where(even, q[0], p[0]), ucat, jnp.where(even, q[2], p[2])) for p, q in zip(near, far)
+    ]
 
     def pair(o, b):
         return remote(accs.at[o, b], pr.at[o, b], p_ss.at[o, b], p_rs.at[o, b], partner)
@@ -249,7 +262,6 @@
             more(o, 1 - c, b)
             accs[o, b] = accm[rows_at(o, 1 - c, b), :].astype(BF16)
             pair(o, b).start()
-        for b in range(B):
             more(o, c, b)
             if o is not y:
                 pair(o, b).wait_recv()
@@ -293,8 +305,7 @@
         bracket = run[at, :]
         for e in range(b):
             bracket = bracket - mm(fac[at, cols(m * B + e)], yb[m * B + e])
-        hi, low = halves(bracket)
-        yb[m * B + b] = (mm(sinv[at, :], hi) + mm(sinv[at, :], low)).astype(BF16)
+        yb[m * B + b] = mm(sinv[at, :], bracket.astype(BF16)).astype(BF16)
         pl.when(m < M - 1)(lambda b=b: forward(m * B + b).start())
     for b in range(B):
         runt[:, b * WSN:(b + 1) * WSN] = yb[m * B + b].astype(F32).T
@@ -312,10 +323,13 @@
         part = xb.at[pl.ds(q * nbs, nbs)]
         return remote(part, part, xu_ss.at[q], xu_rs.at[q], up)
 
-    def send_x(b):
+    def turn_x(b):
         block = xt[:, b * WSN:(b + 1) * WSN].astype(F32).T.astype(BF16)
         q = m * B + b
         xb[pl.ds(q * nbs, nbs)] = block.reshape(nbs, BLK, R)
+
+    def send_x(b):
+        q = m * B + b
         pl.when(m < M - 1)(lambda: xup(q).start())
         pl.when(m > 0)(lambda: xdown(q).start())
 
@@ -330,9 +344,12 @@
         for e in range(b + 1, B):
             rows = pl.ds(e * WSN, WSN)
             bracket = bracket - mm(xt[:, rows], fac[rows, cols(m * B + b)])
-        hi, low = halves(bracket)
-        xt[:, at] = (mm(hi, sinv[at, :]) + mm(low, sinv[at, :])).astype(BF16)
-        pl.when(m == 0)(lambda b=b: send_x(b))
+        xt[:, at] = mm(bracket.astype(BF16), sinv[at, :]).astype(BF16)
+
+        @pl.when(m == 0)
+        def _():
+            turn_x(b)
+            send_x(b)
 
     @pl.loop(0, m * B)
     def _(i):
@@ -345,6 +362,9 @@
 
     @pl.when(m > 0)
     def _():
+        for b in reversed(range(B)):
+            turn_x(b)
+
         @pl.loop(0, m * B)
         def _(q):
             back(q).wait_send()

time: 113 us -> 110 us (0.973)
  Pallas kernels: 108 us -> 105 us
    pallas_call x1, Pallas kernels: 108 us -> 105 us  [shards(): pl.pallas_call(functools.partial(kernel, S, M), out_shape=(jax.ShapeDtype...]
where the time goes in v3:
time: 110 us
  Pallas kernels  105 us (95%)
  local copies, waits for them, and re-layouts  4.13 us (4%)
    pallas_call x1, Pallas kernels, shards(): pl.pallas_call(functools.partial(kernel, S, M), out_shape=(jax.ShapeDtype...  105 us
    unnamed x2, local copies, waits for them, and re-layouts  4.13 us

profile of v3, /device:TPU:13, one launch (start us, length us, event | category | flops | bytes accessed | tf_op | source)
XLA Modules:
  0.0 110.0 jit_solution(11893431412515294921)
XLA Ops:
  0.6 105.2 %shard_map.95 = (bf16[4,512,256]{2,1,0:T(8,128)(2,1)}, bf16[16,64,256]{2,1,0:T(8,128)(2,1)}) custom-call(bf16[4,512,256]{2,1,0:T(8,128)(2,1)} %right_h.1, bf16[4,512,512]{2,1,0:T(8,128)(2,1)} %inv_h.1, bf16[4,256,512]{2,1,0:T(8,128)(2,1)} %panels_h.1, s32[4,4]{1,0:T(4,128)} %block_s.1, s32[4]{0:T(128)} %tree_s.1, bf16[1024,256]{1,0:T(8,128)(2,1)} %sright_h.1, ...), custom_call_target="tpu_custom_call" | custom-call | flops 12000000000 | bytes 16000000 | tf_op jit(solution)/shard_map/pallas_call | solution.py:478
  105.9 2.3 %copy.12 = bf16[4,512,256]{2,1,0:T(8,128)(2,1)} copy(bf16[4,512,256]{2,1,0:T(8,128)(2,1)} %get-tuple-element.8) | data formatting | bytes 2097152
  108.1 1.9 %copy.13 = bf16[1024,256]{1,0:T(8,128)(2,1)} copy(bf16[1024,256]{1,0:T(8,128)(2,1)} %bitcast.1) | data formatting | bytes 1048576

commit v4 on v3

--- a/solution.py
+++ b/solution.py
@@ -83,9 +83,9 @@
         pl.when(cond)(lambda: greet(dev))
         return cond.astype(jnp.int32)
 
-    friends = when_greet(m > 0, down) + when_greet(m < M - 1, up)
-    for i in range(1, ny):
-        greet((s, lax.rem(y + i, ny) * 2 + c))
+    friends = jnp.int32(M - 1)
+    for i in range(1, M):
+        greet((s, lax.rem(m + i, M)))
     for d in (1, 2):
         friends = friends + when_greet(s >= d, (s - d, m))
         friends = friends + when_greet(s + d < S, (s + d, m))
@@ -118,7 +118,7 @@
     mv[...] = meta
     dist, rank = slots(own, s)
 
-    pl.semaphore_wait(barrier, friends + (ny - 1))
+    pl.semaphore_wait(barrier, friends)
 
     def metas(d):
         return remote(mv, mr.at[d - 1], m_ss.at[d - 1], m_rs.at[d - 1], (s - d, m))
@@ -319,9 +319,13 @@
         part = xb.at[pl.ds(q * nbs, nbs)]
         return remote(part, part, xd_ss.at[q], xd_rs.at[q], down)
 
-    def xup(q):
+    def xup(q, to):
         part = xb.at[pl.ds(q * nbs, nbs)]
-        return remote(part, part, xu_ss.at[q], xu_rs.at[q], up)
+        return remote(part, part, xu_ss.at[q, to], xu_rs.at[q], (s, to))
+
+    def later_chips(act):
+        for o in range(1, ny):
+            pl.when(o > y)(lambda o=o: act(2 * o))
 
     def turn_x(b):
         block = xt[:, b * WSN:(b + 1) * WSN].astype(F32).T.astype(BF16)
@@ -330,7 +334,8 @@
 
     def send_x(b):
         q = m * B + b
-        pl.when(m < M - 1)(lambda: xup(q).start())
+        later_chips(lambda to: xup(q, to).start())
+        pl.when(c == 0)(lambda: xup(q, m + 1).start())
         pl.when(m > 0)(lambda: xdown(q).start())
 
     for b in reversed(range(B)):
@@ -383,8 +388,8 @@
     @pl.loop(0, m * B)
     def _(i):
         q = m * B - 1 - i
-        xup(q).wait_recv()
-        pl.when(m < M - 1)(lambda: xup(q).start())
+        xup(q, m).wait_recv()
+        pl.when(c == 0)(lambda: xup(q, m + 1).start())
 
     def pieces(d, third):
         if third:
@@ -437,7 +442,15 @@
         @pl.loop(0, (m + 1) * B)
         def _(q):
             forward(q).wait_send()
-            xup(q).wait_send()
+
+    @pl.when(c == 0)
+    def _():
+        @pl.loop(0, (m + 1) * B)
+        def _(q):
+            xup(q, m + 1).wait_send()
+
+    for b in range(B):
+        later_chips(lambda to, b=b: xup(m * B + b, to).wait_send())
 
     @pl.when(m > 0)
     def _():
@@ -448,6 +461,19 @@
     out_sep.wait()
     for j in range(nl):
         pltpu.make_async_copy(lo.at[j], ox.at[j], osem.at[j]).wait()
+
+
+def write_out(leaf_h, sep_h, ox, osx, sem):
+    nl = leaf_h.shape[0]
+    half = sep_h.shape[0] // 2
+    copies = [pltpu.make_async_copy(leaf_h.at[j], ox.at[j], sem.at[j]) for j in range(nl)]
+    for i in range(2):
+        part = pl.ds(i * half, half)
+        copies.append(pltpu.make_async_copy(sep_h.at[part], osx.at[part], sem.at[nl + i]))
+    for copy in copies:
+        copy.start()
+    for copy in copies:
+        copy.wait()
 
 
 def shards(S, M, leaf_right, leaf_inverse, panels, leaf_subtree, panel_block, separator_right, separator_inverse, separator_factor):
@@ -473,7 +499,7 @@
         V((nslots, KB * BLK, R), BF16), V((2 * nl - 3, KB * BLK, R), BF16), V((nl, W, R), BF16),
         D((3 * nl + 3,)), D((2,)), D((nl + 1,)),
         D((3,)), D((3,)), D((2,)), D((2,)), D((ny, B)), D((ny, B)), D((ny, B)), D((ny, B)),
-        D((N,)), D((N,)), D((N,)), D((N,)), D((N,)), D((N,)), D((N,)), D((N,)), D((3,)), D((3,)),
+        D((N,)), D((N,)), D((N,)), D((N,)), D((N,)), D((N,)), D((N, M)), D((N,)), D((3,)), D((3,)),
     ]
     leaf_x, sep_x = pl.pallas_call(
         functools.partial(kernel, S, M),
@@ -493,6 +519,17 @@
         ),
         cost_estimate=pl.CostEstimate(flops=12_000_000_000, bytes_accessed=16_000_000, transcendentals=0),
     )(leaf_right, leaf_inverse, panels, panel_block, leaf_subtree, separator_right, separator_inverse, separator_factor)
+    leaf_x, sep_x = pl.pallas_call(
+        write_out,
+        out_shape=(
+            jax.ShapeDtypeStruct((nl, W, R), BF16),
+            jax.ShapeDtypeStruct((nbm, BLK, R), BF16),
+        ),
+        in_specs=[anywhere, anywhere],
+        out_specs=(anywhere, anywhere),
+        scratch_shapes=[D((nl + 2,))],
+        cost_estimate=pl.CostEstimate(flops=0, bytes_accessed=3_000_000, transcendentals=0),
+    )(leaf_x, sep_x)
     return leaf_x, sep_x.reshape(SH, R)
 
 

time: 110 us -> 148 us (1.35)
  Pallas kernels: 105 us -> 147 us
  local copies, waits for them, and re-layouts: 4.13 us -> 0 us
    pallas_call x0 -> x1, Pallas kernels: none -> 48.8 us  [shards(): pl.pallas_call(write_out, out_shape=(jax.ShapeDtypeStruct((nl, W, R), BF1...]
    pallas_call x1, Pallas kernels: 105 us -> 98.7 us  [shards(): pl.pallas_call(functools.partial(kernel, S, M), out_shape=(jax.ShapeDtype...]
    unnamed x2 -> x0, local copies, waits for them, and re-layouts: 4.13 us -> none
where the time goes in v4:
time: 148 us
  Pallas kernels  147 us (99%)
    pallas_call x1, Pallas kernels, shards(): pl.pallas_call(functools.partial(kernel, S, M), out_shape=(jax.ShapeDtype...  98.7 us
    pallas_call x1, Pallas kernels, shards(): pl.pallas_call(write_out, out_shape=(jax.ShapeDtypeStruct((nl, W, R), BF1...  48.8 us

profile of v4, /device:TPU:13, one launch (start us, length us, event | category | flops | bytes accessed | tf_op | source)
XLA Modules:
  0.0 148.1 jit_solution(14837357677471622720)
XLA Ops:
  0.6 98.7 %shard_map.95 = (bf16[4,512,256]{2,1,0:T(8,128)(2,1)}, bf16[16,64,256]{2,1,0:T(8,128)(2,1)}) custom-call(bf16[4,512,256]{2,1,0:T(8,128)(2,1)} %right_h.1, bf16[4,512,512]{2,1,0:T(8,128)(2,1)} %inv_h.1, bf16[4,256,512]{2,1,0:T(8,128)(2,1)} %panels_h.1, s32[4,4]{1,0:T(4,128)} %block_s.1, s32[4]{0:T(128)} %tree_s.1, bf16[1024,256]{1,0:T(8,128)(2,1)} %sright_h.1, ...), custom_call_target="tpu_custom_call" | custom-call | flops 12000000000 | bytes 16000000 | tf_op jit(solution)/shard_map/pallas_call | solution.py:504
  99.3 48.8 %shard_map.96 = (bf16[4,512,256]{2,1,0:T(8,128)(2,1)}, bf16[16,64,256]{2,1,0:T(8,128)(2,1)}) custom-call(bf16[4,512,256]{2,1,0:T(8,128)(2,1)} %get-tuple-element.6.leaf_h, bf16[16,64,256]{2,1,0:T(8,128)(2,1)} %get-tuple-element.7.sep_h), custom_call_target="tpu_custom_call" | custom-call | bytes 3000000 | tf_op jit(solution)/shard_map/pallas_call | solution.py:522

commit v5 on v4

--- a/solution.py
+++ b/solution.py
@@ -463,13 +463,13 @@
         pltpu.make_async_copy(lo.at[j], ox.at[j], osem.at[j]).wait()
 
 
-def write_out(leaf_h, sep_h, ox, osx, sem):
-    nl = leaf_h.shape[0]
-    half = sep_h.shape[0] // 2
-    copies = [pltpu.make_async_copy(leaf_h.at[j], ox.at[j], sem.at[j]) for j in range(nl)]
+def write_out(leaf_v, sep_v, ox, osx, sem):
+    nl = leaf_v.shape[0]
+    half = sep_v.shape[0] // 2
+    copies = [pltpu.make_async_copy(leaf_v.at[j], ox.at[j], sem.at[j]) for j in range(nl)]
     for i in range(2):
         part = pl.ds(i * half, half)
-        copies.append(pltpu.make_async_copy(sep_h.at[part], osx.at[part], sem.at[nl + i]))
+        copies.append(pltpu.make_async_copy(sep_v.at[part], osx.at[part], sem.at[nl + i]))
     for copy in copies:
         copy.start()
     for copy in copies:
@@ -525,7 +525,7 @@
             jax.ShapeDtypeStruct((nl, W, R), BF16),
             jax.ShapeDtypeStruct((nbm, BLK, R), BF16),
         ),
-        in_specs=[anywhere, anywhere],
+        in_specs=[pl.BlockSpec(memory_space=pltpu.VMEM)] * 2,
         out_specs=(anywhere, anywhere),
         scratch_shapes=[D((nl + 2,))],
         cost_estimate=pl.CostEstimate(flops=0, bytes_accessed=3_000_000, transcendentals=0),

time: 148 us -> 102 us (0.69)
  Pallas kernels: 147 us -> 101 us
    pallas_call x1, Pallas kernels: 48.8 us -> 2.54 us  [shards(): pl.pallas_call(write_out, out_shape=(jax.ShapeDtypeStruct((nl, W, R), BF1...]
where the time goes in v5:
time: 102 us
  Pallas kernels  101 us (99%)
    pallas_call x1, Pallas kernels, shards(): pl.pallas_call(functools.partial(kernel, S, M), out_shape=(jax.ShapeDtype...  98.7 us
    pallas_call x1, Pallas kernels, shards(): pl.pallas_call(write_out, out_shape=(jax.ShapeDtypeStruct((nl, W, R), BF1...  2.54 us

profile of v5, /device:TPU:13, one launch (start us, length us, event | category | flops | bytes accessed | tf_op | source)
XLA Modules:
  0.0 101.9 jit_solution(2339412762898921445)
XLA Ops:
  0.6 98.7 %shard_map.95 = (bf16[4,512,256]{2,1,0:T(8,128)(2,1)}, bf16[16,64,256]{2,1,0:T(8,128)(2,1)}) custom-call(bf16[4,512,256]{2,1,0:T(8,128)(2,1)} %right_h.1, bf16[4,512,512]{2,1,0:T(8,128)(2,1)} %inv_h.1, bf16[4,256,512]{2,1,0:T(8,128)(2,1)} %panels_h.1, s32[4,4]{1,0:T(4,128)} %block_s.1, s32[4]{0:T(128)} %tree_s.1, bf16[1024,256]{1,0:T(8,128)(2,1)} %sright_h.1, ...), custom_call_target="tpu_custom_call" | custom-call | flops 12000000000 | bytes 16000000 | tf_op jit(solution)/shard_map/pallas_call | solution.py:504
  99.3 2.5 %shard_map.96 = (bf16[4,512,256]{2,1,0:T(8,128)(2,1)}, bf16[16,64,256]{2,1,0:T(8,128)(2,1)}) custom-call(bf16[4,512,256]{2,1,0:T(8,128)(2,1)} %get-tuple-element.6.leaf_v, bf16[16,64,256]{2,1,0:T(8,128)(2,1)} %get-tuple-element.7.sep_v), custom_call_target="tpu_custom_call" | custom-call | bytes 3000000 | tf_op jit(solution)/shard_map/pallas_call | solution.py:522

commit v6 on v5

--- a/solution.py
+++ b/solution.py
@@ -325,7 +325,7 @@
 
     def later_chips(act):
         for o in range(1, ny):
-            pl.when(o > y)(lambda o=o: act(2 * o))
+            pl.when(o > y)(lambda o=o: (act(2 * o + 1), act(2 * o)) and None)
 
     def turn_x(b):
         block = xt[:, b * WSN:(b + 1) * WSN].astype(F32).T.astype(BF16)
@@ -389,7 +389,6 @@
     def _(i):
         q = m * B - 1 - i
         xup(q, m).wait_recv()
-        pl.when(c == 0)(lambda: xup(q, m + 1).start())
 
     def pieces(d, third):
         if third:
@@ -445,7 +444,7 @@
 
     @pl.when(c == 0)
     def _():
-        @pl.loop(0, (m + 1) * B)
+        @pl.loop(m * B, (m + 1) * B)
         def _(q):
             xup(q, m + 1).wait_send()
 

time: 102 us -> 109 us (1.069)
  the two profiles are of different devices: /device:TPU:13 before, /device:TPU:6 now
where the time goes in v6:
time: 109 us
  Pallas kernels  108 us (99%)
    pallas_call x1, Pallas kernels, shards(): pl.pallas_call(functools.partial(kernel, S, M), out_shape=(jax.ShapeDtype...  106 us
    pallas_call x1, Pallas kernels, shards(): pl.pallas_call(write_out, out_shape=(jax.ShapeDtypeStruct((nl, W, R), BF1...  2.54 us

profile of v6, /device:TPU:6, one launch (start us, length us, event | category | flops | bytes accessed | tf_op | source)
XLA Modules:
  0.0 108.9 jit_solution(13025917556871128210)
XLA Ops:
  0.6 105.7 %shard_map.95 = (bf16[4,512,256]{2,1,0:T(8,128)(2,1)}, bf16[16,64,256]{2,1,0:T(8,128)(2,1)}) custom-call(bf16[4,512,256]{2,1,0:T(8,128)(2,1)} %right_h.1, bf16[4,512,512]{2,1,0:T(8,128)(2,1)} %inv_h.1, bf16[4,256,512]{2,1,0:T(8,128)(2,1)} %panels_h.1, s32[4,4]{1,0:T(4,128)} %block_s.1, s32[4]{0:T(128)} %tree_s.1, bf16[1024,256]{1,0:T(8,128)(2,1)} %sright_h.1, ...), custom_call_target="tpu_custom_call" | custom-call | flops 12000000000 | bytes 16000000 | tf_op jit(solution)/shard_map/pallas_call | solution.py:503
  106.3 2.5 %shard_map.96 = (bf16[4,512,256]{2,1,0:T(8,128)(2,1)}, bf16[16,64,256]{2,1,0:T(8,128)(2,1)}) custom-call(bf16[4,512,256]{2,1,0:T(8,128)(2,1)} %get-tuple-element.6.leaf_v, bf16[16,64,256]{2,1,0:T(8,128)(2,1)} %get-tuple-element.7.sep_v), custom_call_target="tpu_custom_call" | custom-call | bytes 3000000 | tf_op jit(solution)/shard_map/pallas_call | solution.py:521
